TPU v7x, 512 devices: a whole 4x4x16 slice. The times are simulated.
512 devices in a mesh: frow: 16 (over z), fcol: 32 (over x, y, core).
Axes of the slice: x: 4, y: 4, z: 16, core: 2. Of those that a mesh axis runs over, the one named last changes fastest.
Arguments:
- strips: bfloat16 [2, 16, 32, 64, 4096], P(None, 'frow', 'fcol'), may hold values from -0.09375 to 0.09375
- facet_window: float32 [16, 32, 256], P('frow', 'fcol'), may hold values from 0.25 to 4
- sub_offset: int32 [12], replicated, may hold values from 0 to 4095
- sub_owner: int32 [12], replicated, may hold values from 0 to 15, as said below
- block_tile: int32 [2048], P(('frow', 'fcol')), may hold values from 0 to 47
- vis_coords: float32 [2, 2048, 512], P(None, ('frow', 'fcol')), may hold values from -0.5 to 0.5
Outputs:
- subgrids: bfloat16 [16, 2, 2, 64, 256], P('frow')
- visibilities: float32 [2, 2048, 512], P(None, ('frow', 'fcol'))
Inputs may be any that keep to these rules, and one draw needn't show every extreme that they name: `sub_owner`: no facet row index owns more than 2 listed subgrids, and one owns exactly 2; facet rows 0 and 15 each own at least one.
All inputs are finite; a program needn't handle non-finite values.
Results may differ from a plain program's by a relative error of at most 0.015.
Values may be sent and summed in bfloat16 or wider, within the bound.
A program may use at most 64 MiB of HBM per device.

v0:
```python
import math

import jax
import jax.numpy as jnp
from jax import lax
from jax.sharding import PartitionSpec as P

TS = 64
CAP = 2


TWO_PI = 2.0 * math.pi


def facet_tables(shift_amount, total_len, contrib_cols):
    columns = jnp.arange(contrib_cols, dtype=jnp.int32)
    sample_points = jnp.arange(total_len, dtype=jnp.int32)
    freq_index = (shift_amount + columns) % total_len
    phase_index = sample_points[:, None] * freq_index[None, :] % total_len
    angles = phase_index.astype(jnp.float32) * (TWO_PI / total_len)
    return jnp.concatenate([jnp.cos(angles), jnp.sin(angles)], axis=1).astype(jnp.bfloat16)


def facet_contrib(strip_rows, window_row, table_one, row_count, col_count):
    product = jnp.dot(strip_rows, table_one, preferred_element_type=jnp.float32)
    real_part = product[:row_count, :col_count] - product[row_count:, col_count:]
    imag_part = product[:row_count, col_count:] + product[row_count:, :col_count]
    return (jnp.stack([real_part, imag_part]) * window_row).astype(jnp.bfloat16)


def owner_slots(sub_owner):
    count = sub_owner.shape[0]
    index = jnp.arange(count, dtype=jnp.int32)
    same = (sub_owner[:, None] == sub_owner[None, :]) & (index[None, :] < index[:, None])
    return jnp.sum(same.astype(jnp.int32), axis=1)


def degrid(tiles, coords, tile_side):
    frequency = jnp.arange(tile_side, dtype=jnp.float32) * TWO_PI
    along_row = frequency[None, :, None] * coords[0][:, None, :]
    along_col = frequency[None, :, None] * coords[1][:, None, :]
    cosine_column = jnp.cos(along_col).astype(jnp.bfloat16)
    sine_column = (-jnp.sin(along_col)).astype(jnp.bfloat16)
    cos_row = jnp.cos(along_row)
    sin_row = -jnp.sin(along_row)
    real_tile = tiles[:, 0]
    imag_tile = tiles[:, 1]

    def batched(left_factor, right_factor):
        return jnp.einsum(
            "xul,xlj->xuj", left_factor, right_factor, preferred_element_type=jnp.float32
        )

    half_real = batched(real_tile, cosine_column) - batched(imag_tile, sine_column)
    half_imag = batched(real_tile, sine_column) + batched(imag_tile, cosine_column)
    vis_real = jnp.sum(cos_row * half_real - sin_row * half_imag, axis=1) / tile_side
    vis_imag = jnp.sum(cos_row * half_imag + sin_row * half_real, axis=1) / tile_side
    return jnp.stack([vis_real, vis_imag])


def cut_tiles(stacked_grids, grid_index, tile_row, tile_col, side):

    def single(index, row_pos, col_pos):
        zero_start = index * 0
        starts = (index, zero_start, row_pos * side, col_pos * side)
        return lax.dynamic_slice(stacked_grids, starts, (1, 2, side, side))[0]

    return jax.vmap(single)(grid_index, tile_row, tile_col)


def on_device(strips, facet_window, sub_offset, sub_owner, block_tile, vis_coords):
    row_count = strips.shape[3]
    length = strips.shape[4]
    columns = facet_window.shape[2]
    count = sub_offset.shape[0]
    frows = lax.axis_size("frow")
    fcols = lax.axis_size("fcol")
    scale = 1.0 / math.sqrt(frows * fcols)
    strip_rows = strips.reshape(2 * row_count, length)
    window_row = facet_window.reshape(columns)

    def one_subgrid(shift_amount):
        return facet_contrib(
            strip_rows, window_row, facet_tables(shift_amount, length, columns), row_count, columns
        )

    contrib = lax.map(one_subgrid, sub_offset)
    slot_of = owner_slots(sub_owner)
    target = sub_owner * CAP + slot_of
    selector = jnp.arange(frows * CAP, dtype=jnp.int32)[:, None] == target[None, :]
    outbound_parts = jnp.dot(
        selector.astype(jnp.bfloat16),
        contrib.reshape(count, -1),
        preferred_element_type=jnp.float32,
    ).astype(jnp.bfloat16)
    outbound_parts = outbound_parts.reshape(frows, CAP, 2, row_count, columns)
    arrived = lax.all_to_all(outbound_parts, "frow", split_axis=0, concat_axis=0, tiled=True)
    partial_sum = jnp.sum(arrived, axis=0, dtype=jnp.float32)
    total = lax.psum(partial_sum, "fcol")
    owned = (total * scale).astype(jnp.bfloat16)
    everyone = lax.all_gather(owned[None], "frow", axis=0, tiled=True)
    flat_grid = everyone.reshape(frows * CAP, 2, row_count, columns)
    tiles_across = columns // TS
    tiles_each = row_count // TS * tiles_across
    sub_index = block_tile // tiles_each
    within = block_tile % tiles_each
    tile_row = within // tiles_across
    tile_col = within % tiles_across
    match = sub_index[:, None] == jnp.arange(count, dtype=jnp.int32)[None, :]
    grid_index = jnp.sum(jnp.where(match, target[None, :], 0), axis=1)
    tiles = cut_tiles(flat_grid, grid_index, tile_row, tile_col, TS)
    visibilities = degrid(tiles, vis_coords, TS)
    return (owned[None], visibilities)


def solution(mesh):
    placed = (
        P(None, "frow", "fcol", None, None),
        P("frow", "fcol", None),
        P(),
        P(),
        P(("frow", "fcol")),
        P(None, ("frow", "fcol"), None),
    )
    return jax.shard_map(
        on_device,
        mesh=mesh,
        in_specs=placed,
        out_specs=(P("frow", None, None, None, None), P(None, ("frow", "fcol"), None)),
        check_vma=False,
    )
```

profile of v0, /device:TPU:1, one launch (start us, length us, event | category | flops | bytes accessed | tf_op | source)
XLA Modules:
  0.0 599.3 jit_solution(8022824065986430794)
XLA Ops:
  7.2 0.9 convert_reduce_fusion.1
  8.8 237.0 %while.12 = (s32[]{:T(128)}, bf16[12,2,64,256]{3,2,1,0:T(8,128)(2,1)S(1)}, s32[12]{0:T(128)}, bf16[128,4096]{1,0:T(8,128)(2,1)}, f32[1,1,256]{2,1,0:T(1,128)}, /*index=5*/s32[]{:T(128)}) while((s32[]{:T(128)}, bf16[12,2,64,256]{3,2,1,0:T(8,128)(2,1)S(1)}, s32[12]{0:T(128)}, bf16[128,4096]{1,0:T(8,128)(2,1)}, f32[1,1,256]{2,1,0:T(1,128)}, ...), condition=%wide.region_2.3_spmd, body=%wide.region_1.2_spmd.sunk | while | flops 562170880 | bytes 14490769 | solution.py:87
  8.8 1.3 dynamic_slice.8
  10.8 16.8 %cosine_convert_fusion.2 = (bf16[4096,256]{1,0:T(8,128)(2,1)S(1)}, bf16[4096,256]{1,0:T(8,128)(2,1)S(1)}) fusion(s32[256]{0:T(256)S(1)} %and_select_fusion.6), kind=kLoop, calls=%fused_computation.12.clone.1 | loop fusion | flops 16777216 | bytes 4195328 | tf_op jit(solution)/shard_map/convert
  27.7 0.8 fusion.74
  28.5 1.3 dynamic_slice.8
  30.5 16.8 %cosine_convert_fusion.2 = (bf16[4096,256]{1,0:T(8,128)(2,1)S(1)}, bf16[4096,256]{1,0:T(8,128)(2,1)S(1)}) fusion(s32[256]{0:T(256)S(1)} %and_select_fusion.6), kind=kLoop, calls=%fused_computation.12.clone.1 | loop fusion | flops 16777216 | bytes 4195328 | tf_op jit(solution)/shard_map/convert
  47.4 0.8 fusion.74
  48.3 1.3 dynamic_slice.8
  50.3 16.8 %cosine_convert_fusion.2 = (bf16[4096,256]{1,0:T(8,128)(2,1)S(1)}, bf16[4096,256]{1,0:T(8,128)(2,1)S(1)}) fusion(s32[256]{0:T(256)S(1)} %and_select_fusion.6), kind=kLoop, calls=%fused_computation.12.clone.1 | loop fusion | flops 16777216 | bytes 4195328 | tf_op jit(solution)/shard_map/convert
  67.2 0.8 fusion.74
  68.1 1.3 dynamic_slice.8
  70.0 16.8 %cosine_convert_fusion.2 = (bf16[4096,256]{1,0:T(8,128)(2,1)S(1)}, bf16[4096,256]{1,0:T(8,128)(2,1)S(1)}) fusion(s32[256]{0:T(256)S(1)} %and_select_fusion.6), kind=kLoop, calls=%fused_computation.12.clone.1 | loop fusion | flops 16777216 | bytes 4195328 | tf_op jit(solution)/shard_map/convert
  86.9 0.8 fusion.74
  87.8 1.3 dynamic_slice.8
  89.8 16.8 %cosine_convert_fusion.2 = (bf16[4096,256]{1,0:T(8,128)(2,1)S(1)}, bf16[4096,256]{1,0:T(8,128)(2,1)S(1)}) fusion(s32[256]{0:T(256)S(1)} %and_select_fusion.6), kind=kLoop, calls=%fused_computation.12.clone.1 | loop fusion | flops 16777216 | bytes 4195328 | tf_op jit(solution)/shard_map/convert
  106.7 0.8 fusion.74
  107.6 1.3 dynamic_slice.8
  109.6 16.8 %cosine_convert_fusion.2 = (bf16[4096,256]{1,0:T(8,128)(2,1)S(1)}, bf16[4096,256]{1,0:T(8,128)(2,1)S(1)}) fusion(s32[256]{0:T(256)S(1)} %and_select_fusion.6), kind=kLoop, calls=%fused_computation.12.clone.1 | loop fusion | flops 16777216 | bytes 4195328 | tf_op jit(solution)/shard_map/convert
  126.4 0.8 fusion.74
  127.3 1.3 dynamic_slice.8
  129.3 16.8 %cosine_convert_fusion.2 = (bf16[4096,256]{1,0:T(8,128)(2,1)S(1)}, bf16[4096,256]{1,0:T(8,128)(2,1)S(1)}) fusion(s32[256]{0:T(256)S(1)} %and_select_fusion.6), kind=kLoop, calls=%fused_computation.12.clone.1 | loop fusion | flops 16777216 | bytes 4195328 | tf_op jit(solution)/shard_map/convert
  146.2 0.8 fusion.74
  147.1 1.3 dynamic_slice.8
  149.1 16.8 %cosine_convert_fusion.2 = (bf16[4096,256]{1,0:T(8,128)(2,1)S(1)}, bf16[4096,256]{1,0:T(8,128)(2,1)S(1)}) fusion(s32[256]{0:T(256)S(1)} %and_select_fusion.6), kind=kLoop, calls=%fused_computation.12.clone.1 | loop fusion | flops 16777216 | bytes 4195328 | tf_op jit(solution)/shard_map/convert
  165.9 0.8 fusion.74
  166.8 1.3 dynamic_slice.8
  168.8 16.8 %cosine_convert_fusion.2 = (bf16[4096,256]{1,0:T(8,128)(2,1)S(1)}, bf16[4096,256]{1,0:T(8,128)(2,1)S(1)}) fusion(s32[256]{0:T(256)S(1)} %and_select_fusion.6), kind=kLoop, calls=%fused_computation.12.clone.1 | loop fusion | flops 16777216 | bytes 4195328 | tf_op jit(solution)/shard_map/convert
  185.7 0.8 fusion.74
  186.6 1.3 dynamic_slice.8
  188.6 16.8 %cosine_convert_fusion.2 = (bf16[4096,256]{1,0:T(8,128)(2,1)S(1)}, bf16[4096,256]{1,0:T(8,128)(2,1)S(1)}) fusion(s32[256]{0:T(256)S(1)} %and_select_fusion.6), kind=kLoop, calls=%fused_computation.12.clone.1 | loop fusion | flops 16777216 | bytes 4195328 | tf_op jit(solution)/shard_map/convert
  205.5 0.8 fusion.74
  206.4 1.3 dynamic_slice.8
  208.3 16.8 %cosine_convert_fusion.2 = (bf16[4096,256]{1,0:T(8,128)(2,1)S(1)}, bf16[4096,256]{1,0:T(8,128)(2,1)S(1)}) fusion(s32[256]{0:T(256)S(1)} %and_select_fusion.6), kind=kLoop, calls=%fused_computation.12.clone.1 | loop fusion | flops 16777216 | bytes 4195328 | tf_op jit(solution)/shard_map/convert
  225.2 0.8 fusion.74
  226.1 1.3 dynamic_slice.8
  228.1 16.8 %cosine_convert_fusion.2 = (bf16[4096,256]{1,0:T(8,128)(2,1)S(1)}, bf16[4096,256]{1,0:T(8,128)(2,1)S(1)}) fusion(s32[256]{0:T(256)S(1)} %and_select_fusion.6), kind=kLoop, calls=%fused_computation.12.clone.1 | loop fusion | flops 16777216 | bytes 4195328 | tf_op jit(solution)/shard_map/convert
  247.7 105.8 %all_to_all.5 = bf16[16,2,2,64,256]{4,3,2,1,0:T(8,128)(2,1)S(1)} all-to-all(bf16[16,2,2,64,256]{4,3,2,1,0:T(8,128)(2,1)S(1)} %bitcast.69), channel_id=1, replica_groups=mesh['frow'=16,'fcol'=32] {'frow'}, dimensions={0} | all-to-all | bytes 4194304 | tf_op jit(solution)/shard_map/all_to_all | solution.py:97
  353.9 1.0 copy.15
  355.2 136.2 %all-reduce.2.cloned.1.call-done = f32[2,2,64,256]{2,1,0,3:T(2,128)} async-done(((f32[2,2,64,256]{2,1,0,3:T(2,128)}), f32[2,2,64,256]{2,1,0,3:T(2,128)}) %all-reduce.2.cloned.1.call-update) | async-done | bytes 262160 | tf_op jit(solution)/shard_map/psum | solution.py:99
  491.4 2.0 multiply_convert_fusion
  493.7 1.3 fusion.66
  495.8 82.7 %all-gather.3.cloned.1.call-done = bf16[32,2,64,256]{2,1,0,3:T(2,128)(2,1)} async-done(((bf16[2,2,64,256]{2,1,0,3:T(2,128)(2,1)}), bf16[32,2,64,256]{2,1,0,3:T(2,128)(2,1)}) %all-gather.3.cloned.1.call-update) | async-done | bytes 2097168 | tf_op jit(solution)/shard_map/all_gather | solution.py:101
  578.5 3.1 gather_fusion
  581.9 1.9 fusion.34
  583.9 1.9 fusion.32
  585.9 1.9 convolution_add_fusion
  587.9 4.0 fusion.22
  (111 shorter events, 14.4 us)
Async XLA Ops:
  7.2 484.2 %all-reduce.2.cloned.1.call-start = ((), (), s32[]{:S(2)}) async-start(), calls=%async_computation.1 | async-start | bytes 1048576 | tf_op jit(solution)/shard_map/psum | solution.py:99
  8.8 18.8 %copy-start.2 = (bf16[128,4096]{1,0:T(8,128)(2,1)S(1)}, bf16[128,4096]{1,0:T(8,128)(2,1)}, u32[]{:S(2)}) copy-start(bf16[128,4096]{1,0:T(8,128)(2,1)} %get-tuple-element.151) | copy-start | bytes 3145732 | tf_op jit(solution)/shard_map/while
  27.6 0.8 copy-start
  28.5 18.9 %copy-start.2 = (bf16[128,4096]{1,0:T(8,128)(2,1)S(1)}, bf16[128,4096]{1,0:T(8,128)(2,1)}, u32[]{:S(2)}) copy-start(bf16[128,4096]{1,0:T(8,128)(2,1)} %get-tuple-element.151) | copy-start | bytes 3145732 | tf_op jit(solution)/shard_map/while
  47.4 0.8 copy-start
  48.3 18.9 %copy-start.2 = (bf16[128,4096]{1,0:T(8,128)(2,1)S(1)}, bf16[128,4096]{1,0:T(8,128)(2,1)}, u32[]{:S(2)}) copy-start(bf16[128,4096]{1,0:T(8,128)(2,1)} %get-tuple-element.151) | copy-start | bytes 3145732 | tf_op jit(solution)/shard_map/while
  67.2 0.8 copy-start
  68.0 18.9 %copy-start.2 = (bf16[128,4096]{1,0:T(8,128)(2,1)S(1)}, bf16[128,4096]{1,0:T(8,128)(2,1)}, u32[]{:S(2)}) copy-start(bf16[128,4096]{1,0:T(8,128)(2,1)} %get-tuple-element.151) | copy-start | bytes 3145732 | tf_op jit(solution)/shard_map/while
  86.9 0.8 copy-start
  87.8 18.9 %copy-start.2 = (bf16[128,4096]{1,0:T(8,128)(2,1)S(1)}, bf16[128,4096]{1,0:T(8,128)(2,1)}, u32[]{:S(2)}) copy-start(bf16[128,4096]{1,0:T(8,128)(2,1)} %get-tuple-element.151) | copy-start | bytes 3145732 | tf_op jit(solution)/shard_map/while
  106.7 0.8 copy-start
  107.6 18.9 %copy-start.2 = (bf16[128,4096]{1,0:T(8,128)(2,1)S(1)}, bf16[128,4096]{1,0:T(8,128)(2,1)}, u32[]{:S(2)}) copy-start(bf16[128,4096]{1,0:T(8,128)(2,1)} %get-tuple-element.151) | copy-start | bytes 3145732 | tf_op jit(solution)/shard_map/while
  126.4 0.8 copy-start
  127.3 18.9 %copy-start.2 = (bf16[128,4096]{1,0:T(8,128)(2,1)S(1)}, bf16[128,4096]{1,0:T(8,128)(2,1)}, u32[]{:S(2)}) copy-start(bf16[128,4096]{1,0:T(8,128)(2,1)} %get-tuple-element.151) | copy-start | bytes 3145732 | tf_op jit(solution)/shard_map/while
  146.2 0.8 copy-start
  147.1 18.9 %copy-start.2 = (bf16[128,4096]{1,0:T(8,128)(2,1)S(1)}, bf16[128,4096]{1,0:T(8,128)(2,1)}, u32[]{:S(2)}) copy-start(bf16[128,4096]{1,0:T(8,128)(2,1)} %get-tuple-element.151) | copy-start | bytes 3145732 | tf_op jit(solution)/shard_map/while
  165.9 0.8 copy-start
  166.8 18.9 %copy-start.2 = (bf16[128,4096]{1,0:T(8,128)(2,1)S(1)}, bf16[128,4096]{1,0:T(8,128)(2,1)}, u32[]{:S(2)}) copy-start(bf16[128,4096]{1,0:T(8,128)(2,1)} %get-tuple-element.151) | copy-start | bytes 3145732 | tf_op jit(solution)/shard_map/while
  185.7 0.8 copy-start
  186.6 18.9 %copy-start.2 = (bf16[128,4096]{1,0:T(8,128)(2,1)S(1)}, bf16[128,4096]{1,0:T(8,128)(2,1)}, u32[]{:S(2)}) copy-start(bf16[128,4096]{1,0:T(8,128)(2,1)} %get-tuple-element.151) | copy-start | bytes 3145732 | tf_op jit(solution)/shard_map/while
  205.4 0.8 copy-start
  206.3 18.9 %copy-start.2 = (bf16[128,4096]{1,0:T(8,128)(2,1)S(1)}, bf16[128,4096]{1,0:T(8,128)(2,1)}, u32[]{:S(2)}) copy-start(bf16[128,4096]{1,0:T(8,128)(2,1)} %get-tuple-element.151) | copy-start | bytes 3145732 | tf_op jit(solution)/shard_map/while
  225.2 0.8 copy-start
  226.1 18.9 %copy-start.2 = (bf16[128,4096]{1,0:T(8,128)(2,1)S(1)}, bf16[128,4096]{1,0:T(8,128)(2,1)}, u32[]{:S(2)}) copy-start(bf16[128,4096]{1,0:T(8,128)(2,1)} %get-tuple-element.151) | copy-start | bytes 3145732 | tf_op jit(solution)/shard_map/while
  245.0 0.8 copy-start
  247.7 245.7 %copy-start.3 = (s32[4]{0:T(128)S(1)}, s32[4]{0:T(128)}, u32[]{:S(2)}) copy-start(s32[4]{0:T(128)} %param.12) | copy-start | bytes 52
  247.7 245.9 %copy-start.1 = (f32[2,4,512]{2,1,0:T(4,128)S(1)}, f32[2,4,512]{2,1,0:T(4,128)}, u32[]{:S(2)}) copy-start(f32[2,4,512]{2,1,0:T(4,128)} %param.13) | copy-start | bytes 49156
  354.9 223.6 %all-gather.3.cloned.1.call-start = ((), (), s32[]{:S(2)}) async-start(), calls=%async_computation.2 | async-start | bytes 4456448 | tf_op jit(solution)/shard_map/all_gather | solution.py:101
Sparse Core Ops, SparseCore 0:
  355.1 136.2 all-reduce.1
  493.6 84.9 all-gather.2
where the time goes:
time: 610 us; the launch traced here: 599 us
  waiting for transfers between devices  219 us (36%)
  other arithmetic  217 us (36%)
  blocking collectives  106 us (17%)
  local copies, waits for them, and re-layouts  22.6 us (4%)
  matrix products  20 us (3%)
  between operations  14.2 us (2%)
    another operation x12, other arithmetic  202 us
    psum x1, waiting for transfers between devices, on_device(): total = lax.psum(partial_sum, 'fcol')  136 us
    all_to_all x1, blocking collectives, on_device(): lax.all_to_all(outbound_parts, 'frow', split_axis=0, concat_axis=0, tiled...  106 us
    all_gather x1, waiting for transfers between devices, on_device(): everyone = lax.all_gather(owned[None], 'frow', axis=0, tiled=True)  82.7 us
    dynamic_slice x12, local copies, waits for them, and re-layouts, on_device(): contrib = lax.map(one_subgrid, sub_offset)  15.9 us
  transfers between devices with their start and end apart: 2, of which 2 were waited for; matrix products, arithmetic and copies ran while one was open for 0% of the time, Pallas kernels for 0%

commit v1 on v0

v1 whole, which is shorter than its diff:
```python
import math

import jax
import jax.numpy as jnp
import numpy as np
from jax import lax
from jax.experimental import pallas as pl
from jax.experimental.pallas import tpu as pltpu
from jax.sharding import PartitionSpec as P

MESH = pl.DeviceIdType.MESH
TS = 64
CAP = 2
ROWS = 64
M = 256
L = 4096
S = 12
RADIX = 16
NB = 4
VB = 512
CHUNKS = 3
GROUP = 32
FAR = 8


def dft_table():
    index = np.arange(M)
    angle = 2.0 * np.pi * ((index[:, None] * index[None, :]) % M) / M
    return np.concatenate([np.cos(angle), np.sin(angle)], axis=1).astype(jnp.bfloat16)


def twiddle_table():
    angle = 2.0 * np.pi * np.arange(RADIX)[:, None] * np.arange(M)[None, :] / L
    return np.stack([np.cos(angle), np.sin(angle)]).astype(np.float32)


def half_turn_polynomials():
    nodes = 0.5 * np.cos(np.pi * (np.arange(400) + 0.5) / 800)
    square = nodes * nodes
    sine = np.polynomial.polynomial.polyfit(square, np.sin(np.pi * nodes) / nodes, 5)
    cosine = np.polynomial.polynomial.polyfit(square, np.cos(np.pi * nodes), 5)
    return [float(v) for v in sine], [float(v) for v in cosine]


SINE, COSINE = half_turn_polynomials()


def turn_cos_sin(turns):
    r = turns - jnp.floor(turns + 0.5)
    u = r * r
    s = jnp.full_like(u, SINE[-1])
    c = jnp.full_like(u, COSINE[-1])
    for a, b in zip(SINE[-2::-1], COSINE[-2::-1]):
        s = s * u + a
        c = c * u + b
    s = s * r
    twice = s + s
    return 1.0 - twice * s, twice * c


def times_root(re, im, power):
    power = power % 16
    if power == 0:
        return re, im
    if power == 4:
        return -im, re
    if power == 8:
        return -re, -im
    if power == 12:
        return im, -re
    c = math.cos(2.0 * math.pi * power / 16)
    s = math.sin(2.0 * math.pi * power / 16)
    if power in (2, 6, 10, 14):
        a = abs(c)
        plus, minus = (re + im) * a, (re - im) * a
        return {2: (minus, plus), 6: (-plus, minus), 10: (-minus, -plus), 14: (plus, -minus)}[power]
    return re * c - im * s, re * s + im * c


def dft4(v):
    (ar, ai), (br, bi), (cr, ci), (dr, di) = v
    pr, pi_, qr, qi = ar + cr, ai + ci, ar - cr, ai - ci
    sr, si, tr, ti = br + dr, bi + di, br - dr, bi - di
    return [(pr + sr, pi_ + si), (qr - ti, qi + tr), (pr - sr, pi_ - si), (qr + ti, qi - tr)]


def dft16(x):
    inner = []
    for low in range(4):
        inner.append(dft4([x[4 * high + low] for high in range(4)]))
    out = [None] * 16
    for c0 in range(4):
        column = [times_root(*inner[low][c0], low * c0) for low in range(4)]
        for c1, value in enumerate(dft4(column)):
            out[4 * c1 + c0] = value
    return out


def kernel(
    off_ref, own_ref, tile_ref, strips_hbm, window_ref, coords_ref, table_ref, twiddle_ref,
    sub_ref, vis_ref,
    strips, zb, xt, con, theirs, merged, near, far, grid, row_phase, col_cos, col_sin,
    load_sem, core_s, core_r, near_s, near_r, far_s, far_r, all_s, all_r, fwd_s, fwd_r,
):
    z = lax.axis_index("frow")
    f = lax.axis_index("fcol")
    core = lax.rem(f, 2)
    chip = f // 2
    x, y = chip // 4, lax.rem(chip, 4)
    side = lax.rem(z, 2)
    ring = z // 2
    sibling = f + 1 - 2 * core

    def loads(part):
        rows = pl.ds(16 * part, 16)
        return pltpu.make_async_copy(strips_hbm.at[:, rows], strips.at[:, rows], load_sem.at[part])

    for part in range(4):
        loads(part).start()

    def partner(k):
        dz, kk = k // 16, lax.rem(k, 16)
        to_x = lax.rem(x + kk // 4, 4)
        to_y = lax.rem(y + lax.rem(kk, 4), 4)
        to_chip = 4 * to_x + to_y
        to_side = lax.rem(side + dz, 2)
        return to_chip, to_side, {"frow": 2 * ring + to_side, "fcol": 2 * to_chip + core}

    def along(k):
        return {"frow": 2 * lax.rem(ring + k, FAR) + side, "fcol": f}

    sib = {"frow": z, "fcol": sibling}
    barrier = pltpu.get_barrier_semaphore()
    pl.semaphore_signal(barrier, inc=1, device_id=sib, device_id_type=MESH)

    @pl.loop(1, GROUP)
    def _(k):
        pl.semaphore_signal(barrier, inc=1, device_id=partner(k)[2], device_id_type=MESH)

    @pl.loop(1, FAR)
    def _(k):
        pl.semaphore_signal(barrier, inc=1, device_id=along(k), device_id_type=MESH)

    def remote(src, dst, send, recv, where):
        return pltpu.make_async_remote_copy(
            src_ref=src, dst_ref=dst, send_sem=send, recv_sem=recv, device_id=where, device_id_type=MESH
        )

    for part in range(4):
        loads(part).wait()
        rows = pl.ds(16 * part, 16)
        low_rows = pl.ds(ROWS + 16 * part, 16)

        @pl.loop(0, 2)
        def _(half):
            lane = pl.multiple_of(half * 128, 128)
            samples = []
            for g in range(RADIX):
                lanes = pl.ds(pl.multiple_of(M * g + lane, 128), 128)
                samples.append((strips[0, rows, lanes].astype(jnp.float32), strips[1, rows, lanes].astype(jnp.float32)))
            first = pl.ds(lane, 128)
            second = pl.ds(pl.multiple_of(M + lane, 128), 128)
            for c, (re, im) in enumerate(dft16(samples)):
                if c:
                    cos = twiddle_ref[0, pl.ds(c, 1), first]
                    sin = twiddle_ref[1, pl.ds(c, 1), first]
                    re, im = re * cos - im * sin, re * sin + im * cos
                re16, im16 = re.astype(jnp.bfloat16), im.astype(jnp.bfloat16)
                zb[c, rows, first] = re16
                zb[c, rows, second] = -im16
                zb[c, low_rows, first] = im16
                zb[c, low_rows, second] = re16

    for pair in range(RADIX // 2):
        both = zb[2 * pair : 2 * pair + 2].reshape(2 * 128, 2 * M)
        product = lax.dot_general(
            table_ref[...], both, (((1,), (1,)), ((), ())), preferred_element_type=jnp.float32
        )
        for e in range(2):
            c = 2 * pair + e
            piece = product[:, 128 * e : 128 * e + 128]
            xt[pl.ds(c, M, stride=RADIX), :] = piece
            xt[pl.ds(L + c, M // RADIX, stride=RADIX), :] = piece[: M // RADIX]

    window = jnp.transpose(jnp.broadcast_to(window_ref[...], (128, M)))

    for j in range(CHUNKS):
        for q in range(4):
            s = 4 * j + q
            con[s] = (xt[pl.ds(off_ref[s], M), :] * window).astype(jnp.bfloat16)
        if j == 0:
            pl.semaphore_wait(barrier, 1 + (GROUP - 1) + (FAR - 1))
        for e in range(2):
            h = 2 * j + e
            remote(con.at[2 * h + 1 - core], theirs.at[h], core_s.at[h], core_r.at[h], sib).start()

    def near_copy(j, k):
        to_chip, to_side, where = partner(k)
        src = merged.at[2 * j + to_side, pl.ds(pl.multiple_of(16 * to_chip, 16), 16)]
        return remote(src, near.at[j, k], near_s.at[j], near_r.at[j], where)

    for j in range(CHUNKS):
        for e in range(2):
            h = 2 * j + e
            remote(con.at[2 * h + 1 - core], theirs.at[h], core_s.at[h], core_r.at[h], sib).wait_recv()
            merged[h] = (con[2 * h + core].astype(jnp.float32) + theirs[h].astype(jnp.float32)).astype(jnp.bfloat16)

        @pl.loop(1, GROUP)
        def _(k):
            near_copy(j, k).start()

    steps = lax.broadcasted_iota(jnp.int32, (TS, 128), 0).astype(jnp.float32)

    @pl.loop(0, VB // 128)
    def _(block):
        lanes = pl.ds(pl.multiple_of(128 * block, 128), 128)
        later = pl.ds(pl.multiple_of(VB + 128 * block, 128), 128)
        for k in range(NB):
            cos, sin = turn_cos_sin(steps * coords_ref[0, k : k + 1, lanes])
            cos, sin = cos.astype(jnp.bfloat16), sin.astype(jnp.bfloat16)
            row_phase[k, 0:TS, lanes] = cos
            row_phase[k, TS : 2 * TS, lanes] = sin
            row_phase[k, 0:TS, later] = -sin
            row_phase[k, TS : 2 * TS, later] = cos
            cos, sin = turn_cos_sin(steps * coords_ref[1, k : k + 1, lanes])
            col_cos[k, :, lanes] = cos
            col_sin[k, :, lanes] = sin

    mine = pl.ds(pl.multiple_of(16 * chip, 16), 16)

    def far_copy(j, k):
        return remote(far.at[j, ring], far.at[j, ring], far_s.at[j], far_r.at[j], along(k))

    def all_copy(j, k):
        at = grid.at[4 * (2 * (2 * j + side) + core) + chip // 4, pl.ds(pl.multiple_of(16 * lax.rem(chip, 4), 16), 16)]
        return remote(at, at, all_s.at[j], all_r.at[j], partner(k)[2])

    def fwd_copy(j, e, half):
        at = grid.at[pl.ds(4 * (2 * (2 * j + e) + half), 4)]
        return remote(at, at, fwd_s.at[j, e], fwd_r.at[j, e], sib)

    def wait_for(buffer, sem):
        pltpu.make_async_copy(buffer, buffer, sem).wait()

    for j in range(CHUNKS):
        wait_for(near.at[j, pl.ds(1, GROUP - 1)], near_r.at[j])
        total = merged[2 * j + side, mine].astype(jnp.float32)
        for k in range(1, GROUP):
            total = total + near[j, k].astype(jnp.float32)
        far[j, ring] = total.astype(jnp.bfloat16)

        @pl.loop(1, FAR)
        def _(k):
            far_copy(j, k).start()

    scale = 1.0 / math.sqrt(512)
    for j in range(CHUNKS):
        wait_for(far.at[j, pl.ds(1, FAR - 1)], far_r.at[j])
        total = far[j, 0].astype(jnp.float32)
        for k in range(1, FAR):
            total = total + far[j, k].astype(jnp.float32)
        grid[4 * (2 * (2 * j + side) + core) + chip // 4, pl.ds(pl.multiple_of(16 * lax.rem(chip, 4), 16), 16)] = (
            total * scale
        ).astype(jnp.bfloat16)

        @pl.loop(1, GROUP)
        def _(k):
            all_copy(j, k).start()

    for j in range(CHUNKS):
        wait_for(near.at[j, pl.ds(1, GROUP - 1)], all_r.at[j])
        for e in range(2):
            fwd_copy(j, e, core).start()

    for j in range(CHUNKS):
        for e in range(2):
            fwd_copy(j, e, 1 - core).wait_recv()

    count = jnp.int32(0)
    place = [jnp.int32(0)] * CAP
    for s in range(S):
        hit = (own_ref[s] == z).astype(jnp.int32)
        for slot in range(CAP):
            place[slot] = place[slot] + jnp.where((hit == 1) & (count == slot), s, 0)
        count = count + hit
    for slot in range(CAP):
        picked = grid[pl.ds(4 * place[slot], 4)].reshape(M, 2 * ROWS).astype(jnp.float32)
        picked = jnp.where(count > slot, picked, 0.0)
        sub_ref[slot] = jnp.transpose(picked).astype(jnp.bfloat16)

    for k in range(NB):
        tile = grid[tile_ref[k]]
        half = jnp.dot(tile, row_phase[k], preferred_element_type=jnp.float32)
        re, im = half[:, :VB], half[:, VB:]
        cos, sin = col_cos[k], col_sin[k]
        vis_ref[0, pl.ds(k, 1)] = jnp.sum(re * cos + im * sin, axis=0, keepdims=True) * (1.0 / TS)
        vis_ref[1, pl.ds(k, 1)] = jnp.sum(im * cos - re * sin, axis=0, keepdims=True) * (1.0 / TS)

    for j in range(CHUNKS):
        for e in range(2):
            h = 2 * j + e
            remote(con.at[2 * h + 1 - core], theirs.at[h], core_s.at[h], core_r.at[h], sib).wait_send()
            fwd_copy(j, e, core).wait_send()
        wait_for(near.at[j, pl.ds(1, GROUP - 1)], near_s.at[j])
        wait_for(far.at[j, pl.ds(1, FAR - 1)], far_s.at[j])
        wait_for(near.at[j, pl.ds(1, GROUP - 1)], all_s.at[j])


def on_device(strips, facet_window, sub_offset, sub_owner, block_tile, vis_coords):
    smem = pl.BlockSpec(memory_space=pltpu.SMEM)
    vmem = pl.BlockSpec(memory_space=pltpu.VMEM)
    dma = pltpu.SemaphoreType.DMA
    bf16, f32 = jnp.bfloat16, jnp.float32
    subgrids, visibilities = pl.pallas_call(
        kernel,
        out_shape=(
            jax.ShapeDtypeStruct((CAP, 2 * ROWS, M), bf16),
            jax.ShapeDtypeStruct((2, NB, VB), f32),
        ),
        in_specs=[smem, smem, smem, pl.BlockSpec(memory_space=pl.ANY), vmem, vmem, vmem, vmem],
        out_specs=(vmem, vmem),
        scratch_shapes=[
            pltpu.VMEM((2, ROWS, L), bf16),
            pltpu.VMEM((RADIX, 2 * ROWS, 2 * M), bf16),
            pltpu.VMEM((L + M, 2 * ROWS), f32),
            pltpu.VMEM((S, M, 2 * ROWS), bf16),
            pltpu.VMEM((S // 2, M, 2 * ROWS), bf16),
            pltpu.VMEM((S // 2, M, 2 * ROWS), bf16),
            pltpu.VMEM((CHUNKS, GROUP, 16, 2 * ROWS), bf16),
            pltpu.VMEM((CHUNKS, FAR, 16, 2 * ROWS), bf16),
            pltpu.VMEM((4 * S, TS, 2 * ROWS), bf16),
            pltpu.VMEM((NB, 2 * TS, 2 * VB), bf16),
            pltpu.VMEM((NB, TS, VB), f32),
            pltpu.VMEM((NB, TS, VB), f32),
            dma((4,)),
            dma((S // 2,)), dma((S // 2,)),
            dma((CHUNKS,)), dma((CHUNKS,)),
            dma((CHUNKS,)), dma((CHUNKS,)),
            dma((CHUNKS,)), dma((CHUNKS,)),
            dma((CHUNKS, 2)), dma((CHUNKS, 2)),
        ],
        compiler_params=pltpu.CompilerParams(
            collective_id=0, has_side_effects=True, vmem_limit_bytes=40 * 2**20
        ),
        name="predict",
    )(
        sub_offset, sub_owner, block_tile, strips.reshape(2, ROWS, L), facet_window.reshape(1, M), vis_coords,
        jnp.asarray(dft_table()), jnp.asarray(twiddle_table()),
    )
    return subgrids.reshape(1, CAP, 2, ROWS, M), visibilities


def solution(mesh):
    placed = (
        P(None, "frow", "fcol", None, None),
        P("frow", "fcol", None),
        P(),
        P(),
        P(("frow", "fcol")),
        P(None, ("frow", "fcol"), None),
    )
    return jax.shard_map(
        on_device,
        mesh=mesh,
        in_specs=placed,
        out_specs=(P("frow", None, None, None, None), P(None, ("frow", "fcol"), None)),
        check_vma=False,
    )
```

time: 610 us -> 48.9 us (0.08); the launches traced: 599 us -> 48.6 us
  waiting for transfers between devices: 219 us -> 0 us
  other arithmetic: 217 us -> 0 us
  blocking collectives: 106 us -> 0 us
  Pallas kernels: 0 us -> 42.3 us
  matrix products: 20 us -> 0 us
  local copies, waits for them, and re-layouts: 22.6 us -> 5.59 us
  between operations: 14.2 us -> 0.68 us
    another operation x25 -> x0, other arithmetic: 203 us -> none
    psum x1 -> x0, waiting for transfers between devices: 136 us -> none  [on_device(): total = lax.psum(partial_sum, 'fcol')]
    all_to_all x1 -> x0, blocking collectives: 106 us -> none  [on_device(): lax.all_to_all(outbound_parts, 'frow', split_axis=0, concat_axis=0, tiled...]
    all_gather x1 -> x0, waiting for transfers between devices: 82.7 us -> none  [on_device(): everyone = lax.all_gather(owned[None], 'frow', axis=0, tiled=True)]
    pallas_call x0 -> x1, Pallas kernels: none -> 42.3 us  [on_device(): pl.pallas_call(kernel, out_shape=(jax.ShapeDtypeStruct((CAP, 2 * ROWS, M)...]
    dot_general x17 -> x0, matrix products: 20 us -> none  [the longest x4 9.73 us: batched(): jnp.einsum('xul,xlj->xuj', left_factor, right_factor, preferred_element_t...]
    dynamic_slice x12 -> x0, local copies, waits for them, and re-layouts: 15.9 us -> none  [on_device(): contrib = lax.map(one_subgrid, sub_offset)]
    select_n x13 -> x0, other arithmetic: 7.85 us -> none  [the longest x12 7.84 us: facet_tables(): freq_index = (shift_amount + columns) % total_len]
  transfers between devices with their start and end apart: 2 -> 0, of which waited for: 2 -> 0; matrix products, arithmetic and copies ran while one was open for 0% -> 0% of each run, Pallas kernels for 0% -> 0%
where the time goes in v1:
time: 48.9 us; the launch traced here: 48.6 us
  Pallas kernels  42.3 us (87%)
  local copies, waits for them, and re-layouts  5.59 us (11%)
  between operations  0.68 us (1%)
    pallas_call x1, Pallas kernels, on_device(): pl.pallas_call(kernel, out_shape=(jax.ShapeDtypeStruct((CAP, 2 * ROWS, M)...  42.3 us
    unnamed x18, local copies, waits for them, and re-layouts  5.59 us

profile of v1, /device:TPU:1, one launch (start us, length us, event | category | flops | bytes accessed | tf_op | source)
XLA Modules:
  0.0 48.6 jit_solution(15961623766015261444)
XLA Ops:
  0.6 0.0 copy-start.6
  0.6 0.0 copy-start.7
  0.7 0.0 copy-start.4
  0.7 0.0 copy-start.5
  0.7 0.6 %copy-done.6 = s32[12]{0:T(128)S(1)} copy-done((s32[12]{0:T(128)S(1)}, s32[12]{0:T(128)}, u32[]{:S(2)}) %copy-start.6) | copy-done | bytes 72
  1.3 0.0 copy-done.7
  1.3 0.0 copy-done.4
  1.3 0.0 copy-done.5
  1.3 0.0 copy-start
  1.3 1.2 %copy-done = bf16[2,1,1,64,4096]{4,3,2,1,0:T(8,128)(2,1)S(1)} copy-done((bf16[2,1,1,64,4096]{4,3,2,1,0:T(8,128)(2,1)S(1)}, bf16[2,1,1,64,4096]{4,3,2,1,0:T(8,128)(2,1)}, u32[]{:S(2)}) %copy-start) | copy-done | bytes 1048600
  2.6 0.0 copy-start.1
  2.6 0.9 %copy-done.1 = bf16[256,512]{1,0:T(8,128)(2,1)S(1)} copy-done((bf16[256,512]{1,0:T(8,128)(2,1)S(1)}, bf16[256,512]{1,0:T(8,128)(2,1)}, u32[]{:S(2)}) %copy-start.1) | copy-done | bytes 262168
  3.5 0.0 copy-start.2
  3.5 0.8 %copy-done.2 = f32[2,16,256]{2,1,0:T(8,128)S(1)} copy-done((f32[2,16,256]{2,1,0:T(8,128)S(1)}, f32[2,16,256]{2,1,0:T(8,128)}, u32[]{:S(2)}) %copy-start.2) | copy-done | bytes 32792
  4.3 0.0 copy-start.3
  4.3 0.7 %copy-done.3 = f32[2,4,512]{2,1,0:T(4,128)S(1)} copy-done((f32[2,4,512]{2,1,0:T(4,128)S(1)}, f32[2,4,512]{2,1,0:T(4,128)}, u32[]{:S(2)}) %copy-start.3) | copy-done | bytes 16408
  5.0 42.3 %predict.1 = (bf16[2,128,256]{2,1,0:T(8,128)(2,1)S(1)}, f32[2,4,512]{2,1,0:T(4,128)S(1)}) custom-call(s32[12]{0:T(128)S(1)} %copy-done.5, s32[12]{0:T(128)S(1)} %copy-done.6, s32[4]{0:T(128)S(1)} %copy-done.7, bf16[2,64,4096]{2,1,0:T(8,128)(2,1)S(1)} %bitcast.3, f32[1,256]{1,0:T(1,128)S(1)} %bitcast.5, f32[2,4,512]{2,1,0:T(4,128)S(1)} %copy-done.3, ...), custom_call_target="tpu_custom_call" | custom-call | tf_op jit(solution)/shard_map/predict/pallas_call | solution.py:314
  47.3 0.7 %copy.12 = bf16[1,2,2,64,256]{4,3,2,1,0:T(8,128)(2,1)} copy(bf16[1,2,2,64,256]{4,3,2,1,0:T(8,128)(2,1)S(1)} %bitcast.4) | data formatting | bytes 262144
  47.9 0.6 %copy.13 = f32[2,4,512]{2,1,0:T(4,128)} copy(f32[2,4,512]{2,1,0:T(4,128)S(1)} %get-tuple-element.9) | data formatting | bytes 32768
Async XLA Ops:
  0.6 0.7 %copy-start.6 = (s32[12]{0:T(128)S(1)}, s32[12]{0:T(128)}, u32[]{:S(2)}) copy-start(s32[12]{0:T(128)} %own_ref.1) | copy-start | bytes 148
  0.6 0.7 %copy-start.7 = (s32[4]{0:T(128)S(1)}, s32[4]{0:T(128)}, u32[]{:S(2)}) copy-start(s32[4]{0:T(128)} %tile_ref.1) | copy-start | bytes 52
  0.7 0.7 %copy-start.4 = (f32[1,1,256]{2,1,0:T(1,128)S(1)}, f32[1,1,256]{2,1,0:T(1,128)}, u32[]{:S(2)}) copy-start(f32[1,1,256]{2,1,0:T(1,128)} %param.9) | copy-start | bytes 3076
  0.7 0.7 %copy-start.5 = (s32[12]{0:T(128)S(1)}, s32[12]{0:T(128)}, u32[]{:S(2)}) copy-start(s32[12]{0:T(128)} %off_ref.1) | copy-start | bytes 148
  1.3 1.2 %copy-start = (bf16[2,1,1,64,4096]{4,3,2,1,0:T(8,128)(2,1)S(1)}, bf16[2,1,1,64,4096]{4,3,2,1,0:T(8,128)(2,1)}, u32[]{:S(2)}) copy-start(bf16[2,1,1,64,4096]{4,3,2,1,0:T(8,128)(2,1)} %param.8) | copy-start | bytes 3145732
  2.6 0.9 %copy-start.1 = (bf16[256,512]{1,0:T(8,128)(2,1)S(1)}, bf16[256,512]{1,0:T(8,128)(2,1)}, u32[]{:S(2)}) copy-start(bf16[256,512]{1,0:T(8,128)(2,1)} %constant.4.clone.table_ref) | copy-start | bytes 786436
  3.5 0.8 %copy-start.2 = (f32[2,16,256]{2,1,0:T(8,128)S(1)}, f32[2,16,256]{2,1,0:T(8,128)}, u32[]{:S(2)}) copy-start(f32[2,16,256]{2,1,0:T(8,128)} %constant.5.clone.twiddle_ref) | copy-start | bytes 98308
  4.3 0.7 %copy-start.3 = (f32[2,4,512]{2,1,0:T(4,128)S(1)}, f32[2,4,512]{2,1,0:T(4,128)}, u32[]{:S(2)}) copy-start(f32[2,4,512]{2,1,0:T(4,128)} %coords_ref.1) | copy-start | bytes 49156

commit v2 on v1

--- a/solution.py
+++ b/solution.py
@@ -21,6 +21,7 @@
 CHUNKS = 3
 GROUP = 32
 FAR = 8
+DIRECT = (2,)
 
 
 def dft_table():
@@ -96,11 +97,15 @@
     return out
 
 
+def far_first(i):
+    return (i + 2) * (1 - i // 2) + (3 - i) * (i // 2)
+
+
 def kernel(
-    off_ref, own_ref, tile_ref, strips_hbm, window_ref, coords_ref, table_ref, twiddle_ref,
+    off_hbm, own_hbm, tile_hbm, strips_hbm, window_hbm, coords_hbm, table_hbm, twiddle_hbm,
     sub_ref, vis_ref,
-    strips, zb, xt, con, theirs, merged, near, far, grid, row_phase, col_cos, col_sin,
-    load_sem, core_s, core_r, near_s, near_r, far_s, far_r, all_s, all_r, fwd_s, fwd_r,
+    off_ref, own_ref, tile_ref, strips, window_ref, coords_ref, table_ref, twiddle_ref, zb, xt, con, theirs, merged, near, far, grid, row_phase, col_cos, col_sin,
+    load_sem, core_s, core_r, near_s, near_r, far_s, far_r, all_s, all_r, fwd_s, fwd_r, oth_s, oth_r,
 ):
     z = lax.axis_index("frow")
     f = lax.axis_index("fcol")
@@ -115,37 +120,60 @@
         rows = pl.ds(16 * part, 16)
         return pltpu.make_async_copy(strips_hbm.at[:, rows], strips.at[:, rows], load_sem.at[part])
 
-    for part in range(4):
+    def whole(src, dst, n):
+        return pltpu.make_async_copy(src, dst, load_sem.at[4 + n])
+
+    twiddles = whole(twiddle_hbm, twiddle_ref, 0)
+    table = whole(table_hbm, table_ref, 1)
+    windows = whole(window_hbm, window_ref, 2)
+    coords = whole(coords_hbm, coords_ref, 3)
+    offsets = whole(off_hbm, off_ref, 4)
+    owners = whole(own_hbm, own_ref, 5)
+    tiles = whole(tile_hbm, tile_ref, 6)
+    loads(0).start()
+    twiddles.start()
+    for part in range(1, 4):
         loads(part).start()
-
-    def partner(k):
-        dz, kk = k // 16, lax.rem(k, 16)
-        to_x = lax.rem(x + kk // 4, 4)
-        to_y = lax.rem(y + lax.rem(kk, 4), 4)
+    table.start()
+
+    def place_of(k):
+        to_x = lax.rem(x + far_first(k // 8), 4)
+        to_y = lax.rem(y + far_first(lax.rem(k // 2, 4)), 4)
         to_chip = 4 * to_x + to_y
-        to_side = lax.rem(side + dz, 2)
-        return to_chip, to_side, {"frow": 2 * ring + to_side, "fcol": 2 * to_chip + core}
+        to_side = lax.rem(side + 1 - lax.rem(k, 2), 2)
+        return to_chip, to_side
+
+    def partner(k, other):
+        to_chip, to_side = place_of(k)
+        to_core = 1 - core if other else core
+        return {"frow": 2 * ring + to_side, "fcol": 2 * to_chip + to_core}
 
     def along(k):
-        return {"frow": 2 * lax.rem(ring + k, FAR) + side, "fcol": f}
+        step = 4 + (k + 1) // 2 * (2 * lax.rem(k + 1, 2) - 1)
+        return {"frow": 2 * lax.rem(ring + step, FAR) + side, "fcol": f}
 
     sib = {"frow": z, "fcol": sibling}
     barrier = pltpu.get_barrier_semaphore()
-    pl.semaphore_signal(barrier, inc=1, device_id=sib, device_id_type=MESH)
-
-    @pl.loop(1, GROUP)
-    def _(k):
-        pl.semaphore_signal(barrier, inc=1, device_id=partner(k)[2], device_id_type=MESH)
-
-    @pl.loop(1, FAR)
+
+    @pl.loop(0, FAR - 1)
     def _(k):
         pl.semaphore_signal(barrier, inc=1, device_id=along(k), device_id_type=MESH)
+
+    @pl.loop(0, GROUP - 1)
+    def _(k):
+        pl.semaphore_signal(barrier, inc=1, device_id=partner(k, 0), device_id_type=MESH)
+        pl.semaphore_signal(barrier, inc=1, device_id=partner(k, 1), device_id_type=MESH)
+
+    pl.semaphore_signal(barrier, inc=1, device_id=sib, device_id_type=MESH)
+    for load in (offsets, windows, coords, owners, tiles):
+        load.start()
 
     def remote(src, dst, send, recv, where):
         return pltpu.make_async_remote_copy(
             src_ref=src, dst_ref=dst, send_sem=send, recv_sem=recv, device_id=where, device_id_type=MESH
         )
 
+    twiddles.wait()
     for part in range(4):
         loads(part).wait()
         rows = pl.ds(16 * part, 16)
@@ -171,6 +199,7 @@
                 zb[c, low_rows, first] = im16
                 zb[c, low_rows, second] = re16
 
+    table.wait()
     for pair in range(RADIX // 2):
         both = zb[2 * pair : 2 * pair + 2].reshape(2 * 128, 2 * M)
         product = lax.dot_general(
@@ -182,6 +211,8 @@
             xt[pl.ds(c, M, stride=RADIX), :] = piece
             xt[pl.ds(L + c, M // RADIX, stride=RADIX), :] = piece[: M // RADIX]
 
+    windows.wait()
+    offsets.wait()
     window = jnp.transpose(jnp.broadcast_to(window_ref[...], (128, M)))
 
     for j in range(CHUNKS):
@@ -189,15 +220,15 @@
             s = 4 * j + q
             con[s] = (xt[pl.ds(off_ref[s], M), :] * window).astype(jnp.bfloat16)
         if j == 0:
-            pl.semaphore_wait(barrier, 1 + (GROUP - 1) + (FAR - 1))
+            pl.semaphore_wait(barrier, 1 + 2 * (GROUP - 1) + (FAR - 1))
         for e in range(2):
             h = 2 * j + e
             remote(con.at[2 * h + 1 - core], theirs.at[h], core_s.at[h], core_r.at[h], sib).start()
 
     def near_copy(j, k):
-        to_chip, to_side, where = partner(k)
+        to_chip, to_side = place_of(k)
         src = merged.at[2 * j + to_side, pl.ds(pl.multiple_of(16 * to_chip, 16), 16)]
-        return remote(src, near.at[j, k], near_s.at[j], near_r.at[j], where)
+        return remote(src, near.at[j, k], near_s.at[j], near_r.at[j], partner(k, 0))
 
     for j in range(CHUNKS):
         for e in range(2):
@@ -205,10 +236,11 @@
             remote(con.at[2 * h + 1 - core], theirs.at[h], core_s.at[h], core_r.at[h], sib).wait_recv()
             merged[h] = (con[2 * h + core].astype(jnp.float32) + theirs[h].astype(jnp.float32)).astype(jnp.bfloat16)
 
-        @pl.loop(1, GROUP)
+        @pl.loop(0, GROUP - 1)
         def _(k):
             near_copy(j, k).start()
 
+    coords.wait()
     steps = lax.broadcasted_iota(jnp.int32, (TS, 128), 0).astype(jnp.float32)
 
     @pl.loop(0, VB // 128)
@@ -231,9 +263,14 @@
     def far_copy(j, k):
         return remote(far.at[j, ring], far.at[j, ring], far_s.at[j], far_r.at[j], along(k))
 
+    def final(j):
+        return grid.at[4 * (2 * (2 * j + side) + core) + chip // 4, pl.ds(pl.multiple_of(16 * lax.rem(chip, 4), 16), 16)]
+
     def all_copy(j, k):
-        at = grid.at[4 * (2 * (2 * j + side) + core) + chip // 4, pl.ds(pl.multiple_of(16 * lax.rem(chip, 4), 16), 16)]
-        return remote(at, at, all_s.at[j], all_r.at[j], partner(k)[2])
+        return remote(final(j), final(j), all_s.at[j], all_r.at[j], partner(k, 0))
+
+    def other_copy(j, where):
+        return remote(final(j), final(j), oth_s.at[j], oth_r.at[j], where)
 
     def fwd_copy(j, e, half):
         at = grid.at[pl.ds(4 * (2 * (2 * j + e) + half), 4)]
@@ -243,19 +280,19 @@
         pltpu.make_async_copy(buffer, buffer, sem).wait()
 
     for j in range(CHUNKS):
-        wait_for(near.at[j, pl.ds(1, GROUP - 1)], near_r.at[j])
+        wait_for(near.at[j, pl.ds(0, GROUP - 1)], near_r.at[j])
         total = merged[2 * j + side, mine].astype(jnp.float32)
-        for k in range(1, GROUP):
+        for k in range(GROUP - 1):
             total = total + near[j, k].astype(jnp.float32)
         far[j, ring] = total.astype(jnp.bfloat16)
 
-        @pl.loop(1, FAR)
+        @pl.loop(0, FAR - 1)
         def _(k):
             far_copy(j, k).start()
 
     scale = 1.0 / math.sqrt(512)
     for j in range(CHUNKS):
-        wait_for(far.at[j, pl.ds(1, FAR - 1)], far_r.at[j])
+        wait_for(far.at[j, pl.ds(0, FAR - 1)], far_r.at[j])
         total = far[j, 0].astype(jnp.float32)
         for k in range(1, FAR):
             total = total + far[j, k].astype(jnp.float32)
@@ -263,19 +300,30 @@
             total * scale
         ).astype(jnp.bfloat16)
 
-        @pl.loop(1, GROUP)
+        @pl.loop(0, GROUP - 1)
         def _(k):
             all_copy(j, k).start()
-
-    for j in range(CHUNKS):
-        wait_for(near.at[j, pl.ds(1, GROUP - 1)], all_r.at[j])
-        for e in range(2):
-            fwd_copy(j, e, core).start()
-
-    for j in range(CHUNKS):
-        for e in range(2):
-            fwd_copy(j, e, 1 - core).wait_recv()
-
+            if j in DIRECT:
+                other_copy(j, partner(k, 1)).start()
+
+        if j in DIRECT:
+            other_copy(j, sib).start()
+
+    for j in range(CHUNKS):
+        wait_for(near.at[j, pl.ds(0, GROUP - 1)], all_r.at[j])
+        if j not in DIRECT:
+            for e in range(2):
+                fwd_copy(j, e, core).start()
+
+    for j in range(CHUNKS):
+        if j in DIRECT:
+            wait_for(grid.at[pl.ds(0, 8)], oth_r.at[j])
+        else:
+            for e in range(2):
+                fwd_copy(j, e, 1 - core).wait_recv()
+
+    owners.wait()
+    tiles.wait()
     count = jnp.int32(0)
     place = [jnp.int32(0)] * CAP
     for s in range(S):
@@ -300,47 +348,57 @@
         for e in range(2):
             h = 2 * j + e
             remote(con.at[2 * h + 1 - core], theirs.at[h], core_s.at[h], core_r.at[h], sib).wait_send()
-            fwd_copy(j, e, core).wait_send()
-        wait_for(near.at[j, pl.ds(1, GROUP - 1)], near_s.at[j])
-        wait_for(far.at[j, pl.ds(1, FAR - 1)], far_s.at[j])
-        wait_for(near.at[j, pl.ds(1, GROUP - 1)], all_s.at[j])
+            if j not in DIRECT:
+                fwd_copy(j, e, core).wait_send()
+        if j in DIRECT:
+            wait_for(grid.at[pl.ds(0, 8)], oth_s.at[j])
+        wait_for(near.at[j, pl.ds(0, GROUP - 1)], near_s.at[j])
+        wait_for(far.at[j, pl.ds(0, FAR - 1)], far_s.at[j])
+        wait_for(near.at[j, pl.ds(0, GROUP - 1)], all_s.at[j])
 
 
 def on_device(strips, facet_window, sub_offset, sub_owner, block_tile, vis_coords):
-    smem = pl.BlockSpec(memory_space=pltpu.SMEM)
     vmem = pl.BlockSpec(memory_space=pltpu.VMEM)
     dma = pltpu.SemaphoreType.DMA
     bf16, f32 = jnp.bfloat16, jnp.float32
     subgrids, visibilities = pl.pallas_call(
         kernel,
         out_shape=(
-            jax.ShapeDtypeStruct((CAP, 2 * ROWS, M), bf16),
-            jax.ShapeDtypeStruct((2, NB, VB), f32),
+            pltpu.VMEM((CAP, 2 * ROWS, M), bf16),
+            pltpu.VMEM((2, NB, VB), f32),
         ),
-        in_specs=[smem, smem, smem, pl.BlockSpec(memory_space=pl.ANY), vmem, vmem, vmem, vmem],
+        in_specs=[pl.BlockSpec(memory_space=pltpu.HBM)] * 8,
         out_specs=(vmem, vmem),
         scratch_shapes=[
+            pltpu.SMEM((S,), jnp.int32),
+            pltpu.SMEM((S,), jnp.int32),
+            pltpu.SMEM((NB,), jnp.int32),
             pltpu.VMEM((2, ROWS, L), bf16),
+            pltpu.VMEM((1, M), f32),
+            pltpu.VMEM((2, NB, VB), f32),
+            pltpu.VMEM((M, 2 * M), bf16),
+            pltpu.VMEM((2, RADIX, M), f32),
             pltpu.VMEM((RADIX, 2 * ROWS, 2 * M), bf16),
             pltpu.VMEM((L + M, 2 * ROWS), f32),
             pltpu.VMEM((S, M, 2 * ROWS), bf16),
             pltpu.VMEM((S // 2, M, 2 * ROWS), bf16),
             pltpu.VMEM((S // 2, M, 2 * ROWS), bf16),
-            pltpu.VMEM((CHUNKS, GROUP, 16, 2 * ROWS), bf16),
+            pltpu.VMEM((CHUNKS, GROUP - 1, 16, 2 * ROWS), bf16),
             pltpu.VMEM((CHUNKS, FAR, 16, 2 * ROWS), bf16),
             pltpu.VMEM((4 * S, TS, 2 * ROWS), bf16),
             pltpu.VMEM((NB, 2 * TS, 2 * VB), bf16),
             pltpu.VMEM((NB, TS, VB), f32),
             pltpu.VMEM((NB, TS, VB), f32),
-            dma((4,)),
+            dma((11,)),
             dma((S // 2,)), dma((S // 2,)),
             dma((CHUNKS,)), dma((CHUNKS,)),
             dma((CHUNKS,)), dma((CHUNKS,)),
             dma((CHUNKS,)), dma((CHUNKS,)),
             dma((CHUNKS, 2)), dma((CHUNKS, 2)),
+            dma((CHUNKS,)), dma((CHUNKS,)),
         ],
         compiler_params=pltpu.CompilerParams(
-            collective_id=0, has_side_effects=True, vmem_limit_bytes=40 * 2**20
+            collective_id=0, has_side_effects=True, vmem_limit_bytes=60 * 2**20
         ),
         name="predict",
     )(

time: 48.9 us -> 42.6 us (0.87)
  local copies, waits for them, and re-layouts: 5.59 us -> 1.26 us
  Pallas kernels: 42.3 us -> 40.6 us
    unnamed x18 -> x2, local copies, waits for them, and re-layouts: 5.59 us -> 1.26 us
    pallas_call x1, Pallas kernels: 42.3 us -> 40.6 us  [on_device(): pl.pallas_call(kernel, out_shape=(pltpu.VMEM((CAP, 2 * ROWS, M), bf16), p...]
where the time goes in v2:
time: 42.6 us; the launch traced here: 42.5 us
  Pallas kernels  40.6 us (95%)
  local copies, waits for them, and re-layouts  1.26 us (3%)
  between operations  0.64 us (2%)
    pallas_call x1, Pallas kernels, on_device(): pl.pallas_call(kernel, out_shape=(pltpu.VMEM((CAP, 2 * ROWS, M), bf16), p...  40.6 us
    unnamed x2, local copies, waits for them, and re-layouts  1.26 us

profile of v2, /device:TPU:1, one launch (start us, length us, event | category | flops | bytes accessed | tf_op | source)
XLA Modules:
  0.0 42.5 jit_solution(3004613813863784994)
XLA Ops:
  0.6 40.6 %predict.1 = (bf16[2,128,256]{2,1,0:T(8,128)(2,1)S(1)}, f32[2,4,512]{2,1,0:T(4,128)S(1)}) custom-call(s32[12]{0:T(128)} %off_hbm.1, s32[12]{0:T(128)} %own_hbm.1, s32[4]{0:T(128)} %tile_hbm.1, bf16[2,64,4096]{2,1,0:T(8,128)(2,1)} %bitcast.4, f32[1,256]{1,0:T(1,128)} %bitcast.5, f32[2,4,512]{2,1,0:T(4,128)} %coords_hbm.1, ...), custom_call_target="tpu_custom_call" | custom-call | tf_op jit(solution)/shard_map/predict/pallas_call | solution.py:364
  41.2 0.7 %copy.12 = bf16[1,2,2,64,256]{4,3,2,1,0:T(8,128)(2,1)} copy(bf16[1,2,2,64,256]{4,3,2,1,0:T(8,128)(2,1)S(1)} %bitcast.3) | data formatting | bytes 262144
  41.9 0.6 %copy.13 = f32[2,4,512]{2,1,0:T(4,128)} copy(f32[2,4,512]{2,1,0:T(4,128)S(1)} %get-tuple-element.7) | data formatting | bytes 32768

commit v3 on v2

--- a/solution.py
+++ b/solution.py
@@ -97,8 +97,12 @@
     return out
 
 
-def far_first(i):
-    return (i + 2) * (1 - i // 2) + (3 - i) * (i // 2)
+def steps_of(step):
+    dx, dy, dz = step
+    return min(dx, 4 - dx) + min(dy, 4 - dy) + dz
+
+
+ORDER = sorted(((dx, dy, dz) for dx in range(4) for dy in range(4) for dz in range(2)), key=steps_of, reverse=True)
 
 
 def kernel(
@@ -136,31 +140,29 @@
         loads(part).start()
     table.start()
 
-    def place_of(k):
-        to_x = lax.rem(x + far_first(k // 8), 4)
-        to_y = lax.rem(y + far_first(lax.rem(k // 2, 4)), 4)
-        to_chip = 4 * to_x + to_y
-        to_side = lax.rem(side + 1 - lax.rem(k, 2), 2)
-        return to_chip, to_side
+    xs = [x] + [lax.rem(x + d, 4) for d in range(1, 4)]
+    ys = [y] + [lax.rem(y + d, 4) for d in range(1, 4)]
+    chips = [[4 * xs[a] + ys[b] for b in range(4)] for a in range(4)]
+    sides = [side, 1 - side]
+    rows_of = [[pl.ds(pl.multiple_of(16 * chips[a][b], 16), 16) for b in range(4)] for a in range(4)]
+    frows = [z, 2 * ring + 1 - side]
+    fcols = [[[2 * chips[a][b] + core, 2 * chips[a][b] + 1 - core] for b in range(4)] for a in range(4)]
 
     def partner(k, other):
-        to_chip, to_side = place_of(k)
-        to_core = 1 - core if other else core
-        return {"frow": 2 * ring + to_side, "fcol": 2 * to_chip + to_core}
+        dx, dy, dz = ORDER[k]
+        return {"frow": frows[dz], "fcol": fcols[dx][dy][other]}
 
     def along(k):
-        step = 4 + (k + 1) // 2 * (2 * lax.rem(k + 1, 2) - 1)
+        step = (4, 3, 5, 2, 6, 1, 7)[k]
         return {"frow": 2 * lax.rem(ring + step, FAR) + side, "fcol": f}
 
     sib = {"frow": z, "fcol": sibling}
     barrier = pltpu.get_barrier_semaphore()
 
-    @pl.loop(0, FAR - 1)
-    def _(k):
+    for k in range(FAR - 1):
         pl.semaphore_signal(barrier, inc=1, device_id=along(k), device_id_type=MESH)
 
-    @pl.loop(0, GROUP - 1)
-    def _(k):
+    for k in range(GROUP - 1):
         pl.semaphore_signal(barrier, inc=1, device_id=partner(k, 0), device_id_type=MESH)
         pl.semaphore_signal(barrier, inc=1, device_id=partner(k, 1), device_id_type=MESH)
 
@@ -226,8 +228,8 @@
             remote(con.at[2 * h + 1 - core], theirs.at[h], core_s.at[h], core_r.at[h], sib).start()
 
     def near_copy(j, k):
-        to_chip, to_side = place_of(k)
-        src = merged.at[2 * j + to_side, pl.ds(pl.multiple_of(16 * to_chip, 16), 16)]
+        dx, dy, dz = ORDER[k]
+        src = merged.at[2 * j + sides[dz], rows_of[dx][dy]]
         return remote(src, near.at[j, k], near_s.at[j], near_r.at[j], partner(k, 0))
 
     for j in range(CHUNKS):
@@ -236,8 +238,7 @@
             remote(con.at[2 * h + 1 - core], theirs.at[h], core_s.at[h], core_r.at[h], sib).wait_recv()
             merged[h] = (con[2 * h + core].astype(jnp.float32) + theirs[h].astype(jnp.float32)).astype(jnp.bfloat16)
 
-        @pl.loop(0, GROUP - 1)
-        def _(k):
+        for k in range(GROUP - 1):
             near_copy(j, k).start()
 
     coords.wait()
@@ -286,8 +287,7 @@
             total = total + near[j, k].astype(jnp.float32)
         far[j, ring] = total.astype(jnp.bfloat16)
 
-        @pl.loop(0, FAR - 1)
-        def _(k):
+        for k in range(FAR - 1):
             far_copy(j, k).start()
 
     scale = 1.0 / math.sqrt(512)
@@ -300,8 +300,7 @@
             total * scale
         ).astype(jnp.bfloat16)
 
-        @pl.loop(0, GROUP - 1)
-        def _(k):
+        for k in range(GROUP - 1):
             all_copy(j, k).start()
             if j in DIRECT:
                 other_copy(j, partner(k, 1)).start()

time: 42.6 us -> 41.6 us (0.977)
  Pallas kernels: 40.6 us -> 39.5 us
    pallas_call x1, Pallas kernels: 40.6 us -> 39.5 us  [on_device(): pl.pallas_call(kernel, out_shape=(pltpu.VMEM((CAP, 2 * ROWS, M), bf16), p...]
where the time goes in v3:
time: 41.6 us; the launch traced here: 41.4 us
  Pallas kernels  39.5 us (95%)
  local copies, waits for them, and re-layouts  1.26 us (3%)
  between operations  0.64 us (2%)
    pallas_call x1, Pallas kernels, on_device(): pl.pallas_call(kernel, out_shape=(pltpu.VMEM((CAP, 2 * ROWS, M), bf16), p...  39.5 us
    unnamed x2, local copies, waits for them, and re-layouts  1.26 us

profile of v3, /device:TPU:1, one launch (start us, length us, event | category | flops | bytes accessed | tf_op | source)
XLA Modules:
  0.0 41.4 jit_solution(1101389870927517974)
XLA Ops:
  0.6 39.5 %predict.1 = (bf16[2,128,256]{2,1,0:T(8,128)(2,1)S(1)}, f32[2,4,512]{2,1,0:T(4,128)S(1)}) custom-call(s32[12]{0:T(128)} %off_hbm.1, s32[12]{0:T(128)} %own_hbm.1, s32[4]{0:T(128)} %tile_hbm.1, bf16[2,64,4096]{2,1,0:T(8,128)(2,1)} %bitcast.4, f32[1,256]{1,0:T(1,128)} %bitcast.5, f32[2,4,512]{2,1,0:T(4,128)} %coords_hbm.1, ...), custom_call_target="tpu_custom_call" | custom-call | tf_op jit(solution)/shard_map/predict/pallas_call | solution.py:363
  40.2 0.7 %copy.12 = bf16[1,2,2,64,256]{4,3,2,1,0:T(8,128)(2,1)} copy(bf16[1,2,2,64,256]{4,3,2,1,0:T(8,128)(2,1)S(1)} %bitcast.3) | data formatting | bytes 262144
  40.8 0.6 %copy.13 = f32[2,4,512]{2,1,0:T(4,128)} copy(f32[2,4,512]{2,1,0:T(4,128)S(1)} %get-tuple-element.7) | data formatting | bytes 32768

commit v4 on v3

--- a/solution.py
+++ b/solution.py
@@ -354,6 +354,17 @@
         wait_for(near.at[j, pl.ds(0, GROUP - 1)], near_s.at[j])
         wait_for(far.at[j, pl.ds(0, FAR - 1)], far_s.at[j])
         wait_for(near.at[j, pl.ds(0, GROUP - 1)], all_s.at[j])
+
+
+def write_out(sub_ref, vis_ref, sub_hbm, vis_hbm, sems):
+    copies = [
+        pltpu.make_async_copy(sub_ref, sub_hbm, sems.at[0]),
+        pltpu.make_async_copy(vis_ref, vis_hbm, sems.at[1]),
+    ]
+    for copy in copies:
+        copy.start()
+    for copy in copies:
+        copy.wait()
 
 
 def on_device(strips, facet_window, sub_offset, sub_owner, block_tile, vis_coords):
@@ -404,6 +415,18 @@
         sub_offset, sub_owner, block_tile, strips.reshape(2, ROWS, L), facet_window.reshape(1, M), vis_coords,
         jnp.asarray(dft_table()), jnp.asarray(twiddle_table()),
     )
+    subgrids, visibilities = pl.pallas_call(
+        write_out,
+        out_shape=(
+            jax.ShapeDtypeStruct((CAP, 2 * ROWS, M), bf16),
+            jax.ShapeDtypeStruct((2, NB, VB), f32),
+        ),
+        in_specs=[vmem, vmem],
+        out_specs=(pl.BlockSpec(memory_space=pltpu.HBM), pl.BlockSpec(memory_space=pltpu.HBM)),
+        scratch_shapes=[dma((2,))],
+        compiler_params=pltpu.CompilerParams(vmem_limit_bytes=2**20),
+        name="write_out",
+    )(subgrids, visibilities)
     return subgrids.reshape(1, CAP, 2, ROWS, M), visibilities
 
 

time: 41.6 us -> 41 us (0.986)
  local copies, waits for them, and re-layouts: 1.26 us -> 0 us
  Pallas kernels: 39.5 us -> 40.2 us
    unnamed x2 -> x0, local copies, waits for them, and re-layouts: 1.26 us -> none
    pallas_call x0 -> x1, Pallas kernels: none -> 0.68 us  [on_device(): pl.pallas_call(write_out, out_shape=(jax.ShapeDtypeStruct((CAP, 2 * ROWS,...]
where the time goes in v4:
time: 41 us; the launch traced here: 40.8 us
  Pallas kernels  40.2 us (98%)
  between operations  0.64 us (2%)
    pallas_call x1, Pallas kernels, on_device(): pl.pallas_call(kernel, out_shape=(pltpu.VMEM((CAP, 2 * ROWS, M), bf16), p...  39.5 us

profile of v4, /device:TPU:1, one launch (start us, length us, event | category | flops | bytes accessed | tf_op | source)
XLA Modules:
  0.0 40.8 jit_solution(9379023873811837191)
XLA Ops:
  0.6 39.5 %predict.1 = (bf16[2,128,256]{2,1,0:T(8,128)(2,1)S(1)}, f32[2,4,512]{2,1,0:T(4,128)S(1)}) custom-call(s32[12]{0:T(128)} %off_hbm.1, s32[12]{0:T(128)} %own_hbm.1, s32[4]{0:T(128)} %tile_hbm.1, bf16[2,64,4096]{2,1,0:T(8,128)(2,1)} %bitcast.3, f32[1,256]{1,0:T(1,128)} %bitcast.4, f32[2,4,512]{2,1,0:T(4,128)} %coords_hbm.1, ...), custom_call_target="tpu_custom_call" | custom-call | tf_op jit(solution)/shard_map/predict/pallas_call | solution.py:374
  40.2 0.7 %write_out.1 = (bf16[2,128,256]{2,1,0:T(8,128)(2,1)}, f32[2,4,512]{2,1,0:T(4,128)}) custom-call(bf16[2,128,256]{2,1,0:T(8,128)(2,1)S(1)} %get-tuple-element.6.sub_ref, f32[2,4,512]{2,1,0:T(4,128)S(1)} %get-tuple-element.7.vis_ref), custom_call_target="tpu_custom_call" | custom-call | tf_op jit(solution)/shard_map/write_out/pallas_call | solution.py:418

commit v5 on v4

--- a/solution.py
+++ b/solution.py
@@ -134,11 +134,6 @@
     offsets = whole(off_hbm, off_ref, 4)
     owners = whole(own_hbm, own_ref, 5)
     tiles = whole(tile_hbm, tile_ref, 6)
-    loads(0).start()
-    twiddles.start()
-    for part in range(1, 4):
-        loads(part).start()
-    table.start()
 
     xs = [x] + [lax.rem(x + d, 4) for d in range(1, 4)]
     ys = [y] + [lax.rem(y + d, 4) for d in range(1, 4)]
@@ -164,9 +159,13 @@
 
     for k in range(GROUP - 1):
         pl.semaphore_signal(barrier, inc=1, device_id=partner(k, 0), device_id_type=MESH)
-        pl.semaphore_signal(barrier, inc=1, device_id=partner(k, 1), device_id_type=MESH)
 
     pl.semaphore_signal(barrier, inc=1, device_id=sib, device_id_type=MESH)
+    loads(0).start()
+    twiddles.start()
+    for part in range(1, 4):
+        loads(part).start()
+    table.start()
     for load in (offsets, windows, coords, owners, tiles):
         load.start()
 
@@ -222,7 +221,7 @@
             s = 4 * j + q
             con[s] = (xt[pl.ds(off_ref[s], M), :] * window).astype(jnp.bfloat16)
         if j == 0:
-            pl.semaphore_wait(barrier, 1 + 2 * (GROUP - 1) + (FAR - 1))
+            pl.semaphore_wait(barrier, 1 + (GROUP - 1) + (FAR - 1))
         for e in range(2):
             h = 2 * j + e
             remote(con.at[2 * h + 1 - core], theirs.at[h], core_s.at[h], core_r.at[h], sib).start()

time: 41 us -> 40.7 us (level)
  no operation moved by 1% of the time
where the time goes in v5:
time: 40.7 us; the launch traced here: 40.6 us
  Pallas kernels  39.9 us (98%)
  between operations  0.64 us (2%)
    pallas_call x1, Pallas kernels, on_device(): pl.pallas_call(kernel, out_shape=(pltpu.VMEM((CAP, 2 * ROWS, M), bf16), p...  39.2 us

profile of v5, /device:TPU:1, one launch (start us, length us, event | category | flops | bytes accessed | tf_op | source)
XLA Modules:
  0.0 40.6 jit_solution(8014651674484629586)
XLA Ops:
  0.6 39.2 %predict.1 = (bf16[2,128,256]{2,1,0:T(8,128)(2,1)S(1)}, f32[2,4,512]{2,1,0:T(4,128)S(1)}) custom-call(s32[12]{0:T(128)} %off_hbm.1, s32[12]{0:T(128)} %own_hbm.1, s32[4]{0:T(128)} %tile_hbm.1, bf16[2,64,4096]{2,1,0:T(8,128)(2,1)} %bitcast.3, f32[1,256]{1,0:T(1,128)} %bitcast.4, f32[2,4,512]{2,1,0:T(4,128)} %coords_hbm.1, ...), custom_call_target="tpu_custom_call" | custom-call | tf_op jit(solution)/shard_map/predict/pallas_call | solution.py:373
  39.9 0.7 %write_out.1 = (bf16[2,128,256]{2,1,0:T(8,128)(2,1)}, f32[2,4,512]{2,1,0:T(4,128)}) custom-call(bf16[2,128,256]{2,1,0:T(8,128)(2,1)S(1)} %get-tuple-element.6.sub_ref, f32[2,4,512]{2,1,0:T(4,128)S(1)} %get-tuple-element.7.vis_ref), custom_call_target="tpu_custom_call" | custom-call | tf_op jit(solution)/shard_map/write_out/pallas_call | solution.py:417

commit v6 on v4

--- a/solution.py
+++ b/solution.py
@@ -302,10 +302,10 @@
 
         for k in range(GROUP - 1):
             all_copy(j, k).start()
-            if j in DIRECT:
+
+        if j in DIRECT:
+            for k in range(GROUP - 1):
                 other_copy(j, partner(k, 1)).start()
-
-        if j in DIRECT:
             other_copy(j, sib).start()
 
     for j in range(CHUNKS):

time: 41 us -> 41 us (level)
  no operation moved by 1% of the time
where the time goes in v6:
time: 41 us; the launch traced here: 40.9 us
  Pallas kernels  40.2 us (98%)
  between operations  0.64 us (2%)
    pallas_call x1, Pallas kernels, on_device(): pl.pallas_call(kernel, out_shape=(pltpu.VMEM((CAP, 2 * ROWS, M), bf16), p...  39.5 us

profile of v6, /device:TPU:1, one launch (start us, length us, event | category | flops | bytes accessed | tf_op | source)
XLA Modules:
  0.0 40.9 jit_solution(11816980799834086557)
XLA Ops:
  0.6 39.5 %predict.1 = (bf16[2,128,256]{2,1,0:T(8,128)(2,1)S(1)}, f32[2,4,512]{2,1,0:T(4,128)S(1)}) custom-call(s32[12]{0:T(128)} %off_hbm.1, s32[12]{0:T(128)} %own_hbm.1, s32[4]{0:T(128)} %tile_hbm.1, bf16[2,64,4096]{2,1,0:T(8,128)(2,1)} %bitcast.3, f32[1,256]{1,0:T(1,128)} %bitcast.4, f32[2,4,512]{2,1,0:T(4,128)} %coords_hbm.1, ...), custom_call_target="tpu_custom_call" | custom-call | tf_op jit(solution)/shard_map/predict/pallas_call | solution.py:374
  40.2 0.7 %write_out.1 = (bf16[2,128,256]{2,1,0:T(8,128)(2,1)}, f32[2,4,512]{2,1,0:T(4,128)}) custom-call(bf16[2,128,256]{2,1,0:T(8,128)(2,1)S(1)} %get-tuple-element.6.sub_ref, f32[2,4,512]{2,1,0:T(4,128)S(1)} %get-tuple-element.7.vis_ref), custom_call_target="tpu_custom_call" | custom-call | tf_op jit(solution)/shard_map/write_out/pallas_call | solution.py:418
